TPU v7x, 256 devices: a whole 4x4x8 slice. The times are simulated.
256 devices in a mesh: dp: 64 (over z, x, y_hi), mp: 4 (over y_lo, core).
Axes of the slice: x: 4, y: 4 (y_hi: 2, y_lo: 2; y = y_hi * 2 + y_lo), z: 8, core: 2. Of those that a mesh axis runs over, the one named last changes fastest.
Arguments:
- query_in: bfloat16 [65536, 3072], P('dp', 'mp'), may hold values from -72 to 72
- key_in: bfloat16 [65536, 3072], P('dp', 'mp'), may hold values from -72 to 72
- value_in: bfloat16 [65536, 3072], P('dp', 'mp'), may hold values from -16 to 16
- grad_out: bfloat16 [65536, 3072], P('dp', 'mp'), may hold values from -100 to 100
- out_weight: bfloat16 [3072, 3072], P('dp', 'mp'), may hold values from -0.109375 to 0.109375
- query_gain: float32 [24, 128], P('mp'), may hold values from 0.5 to 5.2
- key_gain: float32 [24, 128], P('mp'), may hold values from 0.5 to 5.2
Outputs:
- grad_query: bfloat16 [65536, 3072], P('dp', 'mp')
- grad_key: bfloat16 [65536, 3072], P('dp', 'mp')
- grad_value: bfloat16 [65536, 3072], P('dp', 'mp')
- grad_weight: float32 [3072, 3072], P('dp', 'mp')
- grad_query_gain: float32 [24, 128], P('mp')
- grad_key_gain: float32 [24, 128], P('mp')
All inputs are finite; a program needn't handle non-finite values.
Results may differ from a plain program's by a relative error of at most 0.02.
The roundings to bfloat16 on the way count: a program that leaves them out, or rounds other values in their place, can miss the bound.
Values may be sent and summed in bfloat16 or wider, within the bound.
A program may use at most 128 MiB of HBM per device.

v0:
```python
import math

import jax
import jax.numpy as jnp
from jax import lax
from jax.sharding import PartitionSpec as P

PATCH = 256


epsilon = 1e-06


def head_norm(values):
    centred = values - jnp.mean(values, axis=-1, keepdims=True)
    inverse = lax.rsqrt(jnp.mean(centred * centred, axis=-1, keepdims=True) + epsilon)
    return (centred * inverse, inverse)


def norm_back(grad_hat, normed, inverse, gain):
    upper = grad_hat * gain
    spread = jnp.mean(upper * normed, axis=-1, keepdims=True)
    return (upper - jnp.mean(upper, axis=-1, keepdims=True) - normed * spread) * inverse


def per_device(query_in, key_in, value_in, grad_out, out_weight, query_gain, key_gain):
    tokens_here = query_in.shape[0]
    heads_here = query_gain.shape[0]
    depth = query_gain.shape[1]
    images = tokens_here // PATCH
    layout = (images, PATCH, heads_here, depth)
    factor = 1.0 / math.sqrt(depth)
    query_norm, query_inverse = head_norm(query_in.astype(jnp.float32).reshape(layout))
    key_norm, key_inverse = head_norm(key_in.astype(jnp.float32).reshape(layout))
    query_hat = (query_norm * query_gain).astype(jnp.bfloat16)
    key_hat = (key_norm * key_gain).astype(jnp.bfloat16)
    values = value_in.reshape(layout)
    scores = (
        jnp.einsum("iqhd,ikhd->ihqk", query_hat, key_hat, preferred_element_type=jnp.float32)
        * factor
    )
    top = jnp.max(scores, axis=-1, keepdims=True)
    expo = jnp.exp(scores - top)
    probs = expo / jnp.sum(expo, axis=-1, keepdims=True)
    probs_low = probs.astype(jnp.bfloat16)
    attended = jnp.einsum("ihqk,ikhd->iqhd", probs_low, values, preferred_element_type=jnp.float32)
    attended = attended.astype(jnp.bfloat16).reshape(tokens_here, heads_here * depth)
    attended_all = lax.all_gather(attended, "mp", axis=1, tiled=True)
    grad_weight = lax.psum_scatter(
        lax.dot_general(
            attended_all, grad_out, (((0,), (0,)), ((), ())), preferred_element_type=jnp.float32
        ),
        "dp",
        scatter_dimension=0,
        tiled=True,
    )
    partial_sums = lax.dot_general(
        grad_out,
        lax.all_gather(out_weight, "dp", axis=0, tiled=True),
        (((1,), (1,)), ((), ())),
        preferred_element_type=jnp.float32,
    )
    grad_attended = lax.psum_scatter(partial_sums, "mp", scatter_dimension=1, tiled=True).astype(
        jnp.bfloat16
    )
    grad_heads = grad_attended.reshape(layout)
    grad_value = jnp.einsum(
        "ihqk,iqhd->ikhd", probs_low, grad_heads, preferred_element_type=jnp.float32
    ).astype(jnp.bfloat16)
    grad_probs = jnp.einsum(
        "iqhd,ikhd->ihqk", grad_heads, values, preferred_element_type=jnp.float32
    )
    inner = jnp.sum(probs * grad_probs, axis=-1, keepdims=True)
    grad_scores = (probs * (grad_probs - inner) * factor).astype(jnp.bfloat16)
    grad_qhat = jnp.einsum(
        "ihqk,ikhd->iqhd", grad_scores, key_hat, preferred_element_type=jnp.float32
    )
    grad_khat = jnp.einsum(
        "ihqk,iqhd->ikhd", grad_scores, query_hat, preferred_element_type=jnp.float32
    )
    query_local = jnp.sum(grad_qhat * query_norm, axis=(0, 1))
    key_local = jnp.sum(grad_khat * key_norm, axis=(0, 1))
    query_total, key_total = lax.psum((query_local, key_local), "dp")
    grad_query = norm_back(grad_qhat, query_norm, query_inverse, query_gain).astype(jnp.bfloat16)
    grad_key = norm_back(grad_khat, key_norm, key_inverse, key_gain).astype(jnp.bfloat16)
    width_here = heads_here * depth
    return (
        grad_query.reshape(tokens_here, width_here),
        grad_key.reshape(tokens_here, width_here),
        grad_value.reshape(tokens_here, width_here),
        grad_weight,
        query_total,
        key_total,
    )


def solution(mesh):
    placed = (
        P("dp", "mp"),
        P("dp", "mp"),
        P("dp", "mp"),
        P("dp", "mp"),
        P("dp", "mp"),
        P("mp", None),
        P("mp", None),
    )
    return jax.shard_map(
        per_device,
        mesh=mesh,
        in_specs=placed,
        out_specs=(
            P("dp", "mp"),
            P("dp", "mp"),
            P("dp", "mp"),
            P("dp", "mp"),
            P("mp", None),
            P("mp", None),
        ),
        check_vma=False,
    )
```

profile of v0, /device:TPU:9, one launch (start us, length us, event | category | flops | bytes accessed | tf_op | source)
XLA Modules:
  0.0 1145.5 jit_solution(3026726713580276393)
XLA Ops:
  8.0 3.1 copy.82
  11.0 5.2 reshape.100
  20.8 5.2 reshape.98
  37.3 6.9 fusion.41
  44.2 5.7 fusion.28
  54.2 85.9 %all-gather.3.cloned.1.call-done = bf16[3072,768]{1,0:T(8,128)(2,1)} async-done(((bf16[48,768]{1,0:T(8,128)(2,1)}), bf16[3072,768]{1,0:T(8,128)(2,1)}) %all-gather.3.cloned.1.call-update) | async-done | bytes 4718608 | tf_op jit(solution)/shard_map/all_gather | solution.py:59
  140.1 10.3 fusion.46
  150.7 58.8 %all-gather.5.cloned.1.call-done = bf16[1024,3072]{0,1:T(8,128)(2,1)} async-done(((bf16[1024,768]{0,1:T(8,128)(2,1)}), bf16[1024,3072]{0,1:T(8,128)(2,1)}) %all-gather.5.cloned.1.call-update) | async-done | bytes 6291472 | tf_op jit(solution)/shard_map/all_gather | solution.py:48
  209.4 10.0 fusion.47
  219.5 108.9 %reduce-scatter.3.cloned.1.call-done = f32[1024,768]{1,0:T(8,128)} async-done(((f32[1024,3072]{1,0:T(8,128)}), f32[1024,768]{1,0:T(8,128)}) %reduce-scatter.3.cloned.1.call-update) | async-done | bytes 3145744 | tf_op jit(solution)/shard_map/reduce_scatter | solution.py:63
  330.4 2.8 reshape.105
  333.2 2.9 copy.105
  336.1 5.3 fusion.32
  341.4 12.5 %fusion.15 = (f32[6,128]{1,0:T(8,128)S(1)}, f32[4,256,6]{1,2,0:T(8,128)S(1)}, f32[4,256,6]{1,2,0:T(8,128)S(1)}, f32[4,6,128,256]{3,2,1,0:T(8,128)}) fusion(f32[4,256,6]{1,2,0:T(8,128)S(1)} %add_rsqrt_fusion, f32[4,256,6]{1,2,0:T(8,128)S(1)} %copy.83, f32[4,256,6,128]{1,0,3,2:T(4,128)} %reshape.100, f32[6,128]{1,0:T(8,128)S(1)} %copy-done.9, ...), kind=kOutput, calls=%fused_computation.15 | convolution fusion | flops 419948032 | bytes 20576256 | tf_op jit(solution)/shard_map/ihqk,ikhd->iqhd/dot_general | solution.py:75
  353.9 4.3 multiply_convert_fusion.2
  360.8 3.1 copy.175
  364.0 12.6 %fusion.14 = (f32[6,128]{1,0:T(8,128)S(1)}, f32[4,256,6]{1,2,0:T(8,128)S(1)}, f32[4,256,6]{1,2,0:T(8,128)S(1)}, f32[4,6,128,256]{3,2,1,0:T(8,128)}) fusion(f32[4,256,6]{1,2,0:T(8,128)S(1)} %add_rsqrt_fusion.1, f32[4,256,6]{1,2,0:T(8,128)S(1)} %copy.78, f32[4,256,6,128]{1,0,3,2:T(4,128)} %reshape.98, f32[6,128]{1,0:T(8,128)S(1)} %copy-done.10, ...), kind=kOutput, calls=%fused_computation.12 | convolution fusion | flops 419948032 | bytes 20576256 | tf_op jit(solution)/shard_map/ihqk,iqhd->ikhd/dot_general | solution.py:78
  376.6 4.2 multiply_convert_fusion.1
  383.5 3.0 copy.174
  386.5 5.3 fusion.25
  391.8 4.2 copy.122
  396.0 3.0 copy.173
  399.0 159.3 %all-reduce = (f32[6,128]{1,0:T(8,128)}, f32[6,128]{1,0:T(8,128)}) all-reduce(f32[6,128]{1,0:T(8,128)S(1)} %get-tuple-element.26, f32[6,128]{1,0:T(8,128)S(1)} %get-tuple-element.24), channel_id=1, replica_groups=mesh['dp'=64,'mp'=4] {'dp'}, use_global_device_ids=true, to_apply=%region_14.0 | all-reduce | flops 1536 | bytes 12288 | tf_op jit(solution)/shard_map/psum | solution.py:83
  558.4 580.6 %reduce-scatter.5.cloned.1.call-done = f32[48,768]{1,0:T(8,128)} async-done(((f32[3072,768]{1,0:T(8,128)}), f32[48,768]{1,0:T(8,128)}) %reduce-scatter.5.cloned.1.call-update) | async-done | bytes 147472 | tf_op jit(solution)/shard_map/reduce_scatter | solution.py:49
  (52 shorter events, 28.4 us)
Async XLA Ops:
  7.2 133.0 %copy-start = (bf16[1024,768]{1,0:T(8,128)(2,1)S(1)}, bf16[1024,768]{1,0:T(8,128)(2,1)}, u32[]{:S(2)}) copy-start(bf16[1024,768]{1,0:T(8,128)(2,1)} %param.10) | copy-start | bytes 4718596
  7.2 133.0 %all-gather.3.cloned.1.call-start = ((), (), s32[]{:S(2)}) async-start(), calls=%async_computation.2 | async-start | bytes 4792320 | tf_op jit(solution)/shard_map/all_gather | solution.py:59
  7.9 201.5 %all-gather.5.cloned.1.call-start = ((), (), s32[]{:S(2)}) async-start(), calls=%async_computation.4 | async-start | bytes 7864320 | tf_op jit(solution)/shard_map/all_gather | solution.py:48
  16.2 2.5 copy-start.5
  26.0 2.5 copy-start.4
  31.2 2.8 copy-start.2
  31.2 3.8 copy-start.3
  31.2 3.8 copy-start.9
  31.2 3.8 copy-start.10
  37.3 6.9 copy-start.6
  54.2 274.2 %reduce-scatter.3.cloned.1.call-start = ((), (), s32[]{:S(2)}) async-start(), calls=%async_computation.3 | async-start | bytes 15728640 | tf_op jit(solution)/shard_map/reduce_scatter | solution.py:63
  150.4 988.5 %reduce-scatter.5.cloned.1.call-start = ((), (), s32[]{:S(2)}) async-start(), calls=%async_computation.5 | async-start | bytes 9584640 | tf_op jit(solution)/shard_map/reduce_scatter | solution.py:49
  336.1 5.3 copy-start.8
  360.8 3.1 copy-start.7
  386.5 752.5 %copy-start.1 = (bf16[1024,768]{1,0:T(8,128)(2,1)S(1)}, bf16[1024,768]{1,0:T(8,128)(2,1)}, u32[]{:S(2)}) copy-start(bf16[1024,768]{1,0:T(8,128)(2,1)} %param.10) | copy-start | bytes 4718596
Sparse Core Ops, SparseCore 0:
  11.7 128.4 all-gather.2
  142.5 66.8 all-gather.4
  212.1 116.2 reduce-scatter.2
  334.6 804.3 reduce-scatter.4
where the time goes:
time: 1150 us
  waiting for transfers between devices  835 us (73%)
  blocking collectives  159 us (14%)
  matrix products  68.6 us (6%)
  local copies, waits for them, and re-layouts  47.3 us (4%)
  other arithmetic  21 us (2%)
  between operations  13.9 us (1%)
    reduce_scatter x1, waiting for transfers between devices, per_device(): lax.psum_scatter(lax.dot_general(attended_all, grad_out, (((0,), (0,)), (...  581 us
    psum x1, blocking collectives, per_device(): query_total, key_total = lax.psum((query_local, key_local), 'dp')  159 us
    reduce_scatter x1, waiting for transfers between devices, per_device(): lax.psum_scatter(partial_sums, 'mp', scatter_dimension=1, tiled=True)  109 us
    all_gather x1, waiting for transfers between devices, per_device(): lax.all_gather(out_weight, 'dp', axis=0, tiled=True)  85.9 us
    all_gather x1, waiting for transfers between devices, per_device(): attended_all = lax.all_gather(attended, 'mp', axis=1, tiled=True)  58.8 us
  transfers between devices with their start and end apart: 4, of which 4 were waited for; matrix products, arithmetic and copies ran while one was open for 12% of the time, Pallas kernels for 0%

commit v1 on v0

v1 whole, which is shorter than its diff:
```python
import math

import jax
import jax.numpy as jnp
from jax import lax
from jax.experimental import pallas as pl
from jax.experimental.pallas import tpu as pltpu
from jax.sharding import PartitionSpec as P

PATCH = 256
HD = 128
EPS = 1e-06
F32 = jnp.float32
BF16 = jnp.bfloat16
MESH = pl.DeviceIdType.MESH
NZ, NX = 8, 4
FACTOR = 1.0 / math.sqrt(HD)

NN = (((1,), (0,)), ((), ()))
NT = (((1,), (1,)), ((), ()))
TN = (((0,), (0,)), ((), ()))


def dot(a, b, dims):
    return lax.dot_general(a, b, dims, preferred_element_type=F32)


def device(z, x, yh, yl, c):
    return {"dp": (z * NX + x) * 2 + yh, "mp": yl * 2 + c}


def kernel(
    q_hbm, k_hbm, v_hbm, g_hbm, w_hbm, qgain, kgain,
    gq_hbm, gk_hbm, gv_hbm, gw_out, qg_out, kg_out,
    qb, kb, vb, G, W7, P7, attT, qh, kh, qn, kn, probs, gatt,
    raz, rax, rbx, rbz, fin, gacc, gbuf,
    ld_sem, own_sem, out_sem,
    wr_s, wr_r, gy_s, gy_r, gc_s, gc_r, gf_s, gf_r,
    ag_s, ag_r, rs_s, rs_r, fin_s, fin_r, ga_s, ga_r,
):
    dp, mp = lax.axis_index("dp"), lax.axis_index("mp")
    z, x, yh = dp // 8, (dp // 2) % 4, dp % 2
    yl, c = mp // 2, mp % 2
    zl, yb, cb = z // 4, (z // 2) % 2, z % 2
    m_src, zl_src = z // 2, z % 2

    def to_plane(half):
        return zl_src * 4 + yh * 2 + c, x, half, m_src // 2, m_src % 2

    def to_owner(s):
        return mp * 2 + zl, x, yb, s, cb

    def is_me(d):
        same = (d[0] == z) & (d[1] == x) & (d[2] == yh)
        return same & (d[3] == yl) & (d[4] == c)

    rem = lax.rem

    barrier = pltpu.get_barrier_semaphore()

    def greet(d):
        pl.semaphore_signal(barrier, inc=1, device_id=device(*d), device_id_type=MESH)

    j = x * 2 + yh
    for step in range(1, 8):
        greet((rem(z + step, 8), x, yh, yl, c))
        jj = rem(j + step, 8)
        greet((z, jj // 2, jj % 2, yl, c))
    greet((z, x, yh, 1 - yl, c))
    greet((z, x, yh, yl, 1 - c))
    count = jnp.int32(20)
    for d in (to_plane(0), to_plane(1), to_owner(0), to_owner(1)):
        mine = is_me(d)
        count = count - mine.astype(jnp.int32)
        pl.when(jnp.logical_not(mine))(lambda d=d: greet(d))

    def load(a, i):
        src, dst = ((q_hbm, qb), (k_hbm, kb), (v_hbm, vb))[a]
        rows = pl.ds(i * PATCH, PATCH)
        return pltpu.make_async_copy(src.at[rows], dst.at[rows], ld_sem.at[a, i])

    for i in range(4):
        for a in range(3):
            load(a, i).start()
    own_load = pltpu.make_async_copy(g_hbm, G.at[mp], own_sem)
    own_load.start()
    pl.semaphore_wait(barrier, count)

    def remote(src, dst, send, recv, d):
        return pltpu.make_async_remote_copy(
            src_ref=src, dst_ref=dst, send_sem=send, recv_sem=recv,
            device_id=device(*d), device_id_type=MESH,
        )

    def w_copy(half):
        return remote(w_hbm, W7.at[yl, c, zl_src, x, yh], wr_s.at[half], wr_r.at[yl], to_plane(half))

    for half in range(2):
        mine = is_me(to_plane(half))
        pl.when(jnp.logical_not(mine))(lambda half=half: w_copy(half).start())
        pl.when(mine)(
            lambda: pltpu.make_async_copy(
                w_hbm, W7.at[yl, c, zl_src, x, yh], wr_r.at[yl]
            ).start()
        )

    def w_arrive(s):
        here = W7.at[s, cb, zl, x, yb]
        pltpu.make_async_copy(here, here, wr_r.at[s]).wait()

    def g_rows(ref, i):
        return ref.at[pl.ds(i * PATCH, PATCH)]

    def gy(i, block):
        return remote(g_rows(g_hbm, i), g_rows(G.at[block], i), gy_s.at[i], gy_r.at[i], (z, x, yh, 1 - yl, c))

    def gc(i, block):
        return remote(g_rows(g_hbm, i), g_rows(G.at[block], i), gc_s.at[i], gc_r.at[i], (z, x, yh, yl, 1 - c))

    def gf(i, block):
        part = g_rows(G.at[block], i)
        return remote(part, part, gf_s.at[i], gf_r.at[i], (z, x, yh, yl, 1 - c))

    near = (1 - yl) * 2 + c
    core = yl * 2 + 1 - c
    far = (1 - yl) * 2 + 1 - c
    for i in range(4):
        gy(i, mp).start()
    for i in range(4):
        gc(i, mp).start()

    def g_forward(i):
        gy(i, near).wait_recv()
        gf(i, near).start()

    def half_of(ref, which):
        lead = (slice(None),) * (len(ref.shape) - 1)
        return ref.at[lead + (pl.ds(which * 384, 384),)]

    def side(st):
        return yl if st == 0 else 1 - yl

    def view(ref, st, axis, wide, idx):
        s = side(st)
        if axis == "z":
            a, b, d = idx // 4, (idx // 2) % 2, idx % 2
            return ref.at[s, d, a, :, b] if wide else ref.at[s, d, a, x, b]
        return ref.at[s, :, :, idx, :] if wide else ref.at[s, cb, zl, idx, yb]

    def ring(axis):
        return (NZ, z) if axis == "z" else (NX, x)

    def neighbour(axis, way):
        if axis == "z":
            return rem(z + way + NZ, NZ), x, yh, yl, c
        return z, rem(x + way + NX, NX), yh, yl, c

    AG = ((("x", False), ("z", True)), (("z", False), ("x", True)))

    def ag_part(st, ph, way, step, back):
        axis, wide = AG[st][ph]
        n, me = ring(axis)
        ref = view(W7, st, axis, wide, rem(me - way * back + 2 * n, n))
        return half_of(ref, 0 if way > 0 else 1) if step == n // 2 - 1 else ref

    def ag_copy(st, ph, way, step, back):
        ref = ag_part(st, ph, way, step, back)
        k = 0 if way > 0 else 1
        return remote(
            ref, ref, ag_s.at[st, ph, k, step], ag_r.at[st, ph, k, step], neighbour(AG[st][ph][0], way)
        )

    def ag_send(st, ph, step):
        for way in (1, -1):
            ag_copy(st, ph, way, step, step).start()

    def ag_event(st, ph, step):
        steps = ring(AG[st][ph][0])[0] // 2
        for way in (1, -1):
            ag_copy(st, ph, way, step, step + 1).wait_recv()
            if step + 1 < steps:
                ag_copy(st, ph, way, step + 1, step + 1).start()
        if step + 1 == steps and ph == 0:
            ag_send(st, 1, 0)

    RS = ((("z", True), ("x", False)), (("x", True), ("z", False)))
    landing = ((raz, rax), (rbx, rbz))

    def rs_copy(st, ph, way, step, off):
        axis, wide = RS[st][ph]
        n, me = ring(axis)
        k = 0 if way > 0 else 1
        ref = view(P7, st, axis, wide, rem(me + way * off + 2 * n, n))
        dst = landing[st][ph].at[k, step]
        if step == 0:
            ref, dst = half_of(ref, k), half_of(dst, k)
        return remote(ref, dst, rs_s.at[st, ph, k, step], rs_r.at[st, ph, k, step], neighbour(axis, way))

    def rs_send(st, ph, step):
        axis = RS[st][ph][0]
        for way in (1, -1):
            rs_copy(st, ph, way, step, ring(axis)[0] // 2 - step).start()

    def rs_add(st, ph, way, step, off):
        axis, wide = RS[st][ph]
        n, me = ring(axis)
        k = 0 if way > 0 else 1
        ref = view(P7, st, axis, wide, rem(me + way * off + 2 * n, n))
        got = landing[st][ph].at[k, step]
        if step == 0:
            ref, got = half_of(ref, k), half_of(got, k)

        def add(a, b):
            a[...] = (a[...].astype(F32) + b[...].astype(F32)).astype(BF16)

        if not wide:
            add(ref, got)
        elif axis == "z":
            def body(t, carry):
                add(ref.at[t], got.at[t])
                return carry
            lax.fori_loop(0, NX, body, 0)
        else:
            def body(t, carry):
                add(ref.at[t // 4, (t // 2) % 2, t % 2], got.at[t // 4, (t // 2) % 2, t % 2])
                return carry
            lax.fori_loop(0, NZ, body, 0)

    def fin_copy(st):
        s = side(st)
        return remote(P7.at[s, cb, zl, x, yb], fin.at[yh], fin_s.at[st], fin_r.at[yh], to_owner(s))

    def rs_event(st, ph, step):
        axis = RS[st][ph][0]
        steps = ring(axis)[0] // 2
        for way in (1, -1):
            rs_copy(st, ph, way, step, steps - 1 - step).wait_recv()
            rs_add(st, ph, way, step, steps - 1 - step)
            if step + 1 < steps:
                rs_copy(st, ph, way, step + 1, steps - 1 - step).start()
        if step + 1 == steps:
            if ph == 0:
                rs_send(st, 1, 0)
            else:
                s = side(st)
                mine = is_me(to_owner(s))
                pl.when(jnp.logical_not(mine))(lambda: fin_copy(st).start())
                pl.when(mine)(
                    lambda: pltpu.make_async_copy(
                        P7.at[s, cb, zl, x, yb], fin.at[yh], fin_r.at[yh]
                    ).start()
                )

    def normed(ref, gains, h, rows, cols):
        v = ref[rows, cols].astype(F32)
        v = v - jnp.mean(v, axis=-1, keepdims=True)
        inverse = lax.rsqrt(jnp.mean(v * v, axis=-1, keepdims=True) + EPS)
        return v * inverse, inverse

    def place(it):
        i, h = it // 6, it % 6
        rows = pl.ds(pl.multiple_of(i * PATCH, PATCH), PATCH)
        cols = pl.ds(pl.multiple_of(h * HD, HD), HD)
        return i, h, rows, cols

    def forward(it):
        i, h, rows, cols = place(it)
        a, _ = normed(qb, qgain, h, rows, cols)
        b, _ = normed(kb, kgain, h, rows, cols)
        a_hat = (a * qgain[pl.ds(h, 1), :]).astype(BF16)
        b_hat = (b * kgain[pl.ds(h, 1), :]).astype(BF16)
        qh[rows, cols] = a_hat
        kh[rows, cols] = b_hat
        scores = dot(b_hat, a_hat, NT) * FACTOR
        expo = jnp.exp(scores - jnp.max(scores, axis=0, keepdims=True))
        p = expo * (1.0 / jnp.sum(expo, axis=0, keepdims=True))
        probs[it] = p
        att = dot(vb[rows, cols], p.astype(BF16), TN)
        attT[cols, rows] = att.astype(BF16)

    def back(grad, normal, inverse, gain):
        u = grad * gain
        spread = jnp.mean(u * normal, axis=-1, keepdims=True)
        return (u - jnp.mean(u, axis=-1, keepdims=True) - normal * spread) * inverse

    def backward(it):
        i, h, rows, cols = place(it)
        ga = gatt[rows, cols]
        p = probs[it]
        vals = vb[rows, cols]
        gp = dot(vals, ga, NT)
        inner = jnp.sum(p * gp, axis=0, keepdims=True)
        gs = (p * (gp - inner) * FACTOR).astype(BF16)
        vb[rows, cols] = dot(p.astype(BF16), ga, NN).astype(BF16)
        gk = dot(gs, qh[rows, cols], NN)
        gq = dot(gs, kh[rows, cols], TN)
        a, a_inv = normed(qb, qgain, h, rows, cols)
        b, b_inv = normed(kb, kgain, h, rows, cols)
        gacc[0, pl.ds(h, 1), :] += jnp.sum(gq * a, axis=0, keepdims=True)
        gacc[0, pl.ds(8 + h, 1), :] += jnp.sum(gk * b, axis=0, keepdims=True)
        qb[rows, cols] = back(gq, a, a_inv, qgain[pl.ds(h, 1), :]).astype(BF16)
        kb[rows, cols] = back(gk, b, b_inv, kgain[pl.ds(h, 1), :]).astype(BF16)

    def weight_partial(block):
        s, d = block // 2, block % 2

        def body(t, carry):
            rows = pl.ds(pl.multiple_of(t * 384, 128), 384)
            part = dot(attT[rows, :], G[block], NN).astype(BF16)
            P7[s, d, t] = part.reshape(4, 2, 48, 768)
            return carry

        lax.fori_loop(0, 2, body, 0)

    def attended_grad(t):
        rows = pl.ds(pl.multiple_of(t * 512, 512), 512)
        total = None
        for block in range(4):
            w = W7[block // 2, block % 2].reshape(768, 768)
            part = dot(G[block, rows, :], w, NT)
            total = part if total is None else total + part
        gatt[rows, :] = total.astype(BF16)

    def store(a, i):
        src, dst = ((qb, gq_hbm), (kb, gk_hbm), (vb, gv_hbm))[a]
        rows = pl.ds(i * PATCH, PATCH)
        return pltpu.make_async_copy(src.at[rows], dst.at[rows], out_sem.at[a, i])

    def start_gather():
        for s in range(2):
            w_arrive(s)
        ag_send(0, 0, 0)
        ag_send(1, 0, 0)

    first = {
        1: [start_gather],
        4: [lambda: ag_event(0, 0, 0), lambda: ag_event(1, 0, 0)],
        8: [lambda: ag_event(0, 0, 1), lambda: ag_event(1, 0, 1)],
        12: [lambda: g_forward(0)],
        14: [lambda: ag_event(1, 0, 2)],
        18: [lambda: ag_event(1, 0, 3)],
    }

    def first_body(it, carry):
        for i in range(4):
            @pl.when(it == i * 6)
            def _():
                for a in range(3):
                    load(a, i).wait()
        forward(it)
        for at, events in first.items():
            @pl.when(it == at)
            def _():
                for event in events:
                    event()
        return carry

    lax.fori_loop(0, 24, first_body, 0)
    own_load.wait()
    weight_partial(mp)
    ag_event(0, 1, 0)
    g_forward(1)
    for i in range(4):
        gc(i, core).wait_recv()
    weight_partial(core)
    ag_event(0, 1, 1)
    g_forward(2)
    ag_event(1, 1, 0)
    ag_event(0, 1, 2)
    rs_send(0, 0, 0)
    ag_event(1, 1, 1)
    g_forward(3)
    rs_event(0, 0, 0)
    weight_partial(near)
    for i in range(4):
        gf(i, far).wait_recv()
    weight_partial(far)
    rs_send(1, 0, 0)
    ag_event(0, 1, 3)
    gacc[...] = jnp.zeros_like(gacc)

    second = {
        2: [lambda: rs_event(0, 0, 1)],
        6: [lambda: rs_event(1, 0, 0)],
        10: [lambda: rs_event(0, 0, 2)],
        16: [lambda: rs_event(0, 0, 3)],
        19: [lambda: rs_event(0, 1, 0)],
        22: [lambda: rs_event(0, 1, 1)],
    }

    def second_body(it, carry):
        for t in range(2):
            pl.when(it == t * 12)(lambda t=t: attended_grad(t))
        backward(it)
        for i in range(4):
            @pl.when(it == i * 6 + 5)
            def _():
                for a in range(3):
                    store(a, i).start()
        for at, events in second.items():
            @pl.when(it == at)
            def _():
                for event in events:
                    event()
        return carry

    lax.fori_loop(0, 24, second_body, 0)

    def gain_copy(ph, step):
        if ph == 0:
            jj = rem(j + step, 8)
            d = (z, jj // 2, jj % 2, yl, c)
        else:
            d = (rem(z + step, 8), x, yh, yl, c)
        return remote(
            gacc.at[ph], gbuf.at[ph, step - 1], ga_s.at[ph, step - 1], ga_r.at[ph, step - 1], d
        )

    def gain_send(ph):
        for step in range(1, 8):
            gain_copy(ph, step).start()

    def gain_sum(ph):
        total = gacc[ph]
        for step in range(1, 8):
            gain_copy(ph, step).wait_recv()
            total = total + gbuf[ph, step - 1]
        return total

    gain_send(0)
    rs_event(1, 0, 1)
    gacc[1] = gain_sum(0)
    gain_send(1)
    rs_event(1, 1, 0)
    rs_event(1, 1, 1)
    gains = gain_sum(1)
    qg_out[...] = gains[0:6]
    kg_out[...] = gains[8:14]
    rs_event(1, 1, 2)
    rs_event(1, 1, 3)

    for half in range(2):
        pl.when(jnp.logical_not(is_me(to_plane(half))))(lambda half=half: w_copy(half).wait_send())
    for i in range(4):
        gy(i, mp).wait_send()
        gc(i, mp).wait_send()
        gf(i, near).wait_send()
    for st in range(2):
        for ph in range(2):
            steps = ring(AG[st][ph][0])[0] // 2
            for step in range(steps):
                for way in (1, -1):
                    ag_copy(st, ph, way, step, step).wait_send()
            steps = ring(RS[st][ph][0])[0] // 2
            for step in range(steps):
                for way in (1, -1):
                    rs_copy(st, ph, way, step, steps - step).wait_send()
    for ph in range(2):
        for step in range(1, 8):
            gain_copy(ph, step).wait_send()
    for i in range(4):
        for a in range(3):
            store(a, i).wait()
    for half in range(2):
        pltpu.make_async_copy(fin.at[half], fin.at[half], fin_r.at[half]).wait()
    for st in range(2):
        pl.when(jnp.logical_not(is_me(to_owner(side(st)))))(lambda st=st: fin_copy(st).wait_send())
    gw_out[...] = fin[0].astype(F32) + fin[1].astype(F32)


def per_device(query_in, key_in, value_in, grad_out, out_weight, query_gain, key_gain):
    vmem = pl.BlockSpec(memory_space=pltpu.VMEM)
    anywhere = pl.BlockSpec(memory_space=pl.ANY)
    tokens = jax.ShapeDtypeStruct((1024, 768), BF16)
    dma = pltpu.SemaphoreType.DMA
    act = pltpu.VMEM((1024, 768), BF16)
    big = pltpu.VMEM((2, 2, 2, 4, 2, 48, 768), BF16)
    return pl.pallas_call(
        kernel,
        out_shape=(
            tokens, tokens, tokens,
            jax.ShapeDtypeStruct((48, 768), F32),
            jax.ShapeDtypeStruct((6, 128), F32),
            jax.ShapeDtypeStruct((6, 128), F32),
        ),
        in_specs=[anywhere] * 5 + [vmem] * 2,
        out_specs=(anywhere,) * 3 + (vmem,) * 3,
        scratch_shapes=[
            act, act, act,
            pltpu.VMEM((4, 1024, 768), BF16),
            big, big,
            pltpu.VMEM((768, 1024), BF16),
            act, act,
            pltpu.VMEM((8, 128), F32), pltpu.VMEM((8, 128), F32),
            pltpu.VMEM((24, 256, 256), F32),
            act,
            pltpu.VMEM((2, 4, 4, 48, 768), BF16),
            pltpu.VMEM((2, 2, 48, 768), BF16),
            pltpu.VMEM((2, 2, 2, 2, 2, 48, 768), BF16),
            pltpu.VMEM((2, 4, 48, 768), BF16),
            pltpu.VMEM((2, 48, 768), BF16),
            pltpu.VMEM((2, 16, 128), F32),
            pltpu.VMEM((2, 7, 16, 128), F32),
            dma((3, 4)), dma, dma((3, 4)),
            dma((2,)), dma((2,)), dma((4,)), dma((4,)), dma((4,)), dma((4,)), dma((4,)), dma((4,)),
            dma((2, 2, 2, 4)), dma((2, 2, 2, 4)), dma((2, 2, 2, 4)), dma((2, 2, 2, 4)),
            dma((2,)), dma((2,)), dma((2, 7)), dma((2, 7)),
        ],
        compiler_params=pltpu.CompilerParams(
            collective_id=0, has_side_effects=True, vmem_limit_bytes=60 * 2**20
        ),
        cost_estimate=pl.CostEstimate(flops=12 * 10**9, bytes_accessed=12 * 10**6, transcendentals=1600000),
    )(query_in, key_in, value_in, grad_out, out_weight, query_gain, key_gain)


def solution(mesh):
    rows = P("dp", "mp")
    heads = P("mp", None)
    return jax.shard_map(
        per_device,
        mesh=mesh,
        in_specs=(rows, rows, rows, rows, rows, heads, heads),
        out_specs=(rows, rows, rows, rows, heads, heads),
        check_vma=False,
    )
```

time: 1150 us -> 135 us (0.12)
  waiting for transfers between devices: 835 us -> 0 us
  blocking collectives: 159 us -> 0 us
  Pallas kernels: 0 us -> 125 us
  matrix products: 68.6 us -> 0 us
  local copies, waits for them, and re-layouts: 47.3 us -> 7.75 us
  other arithmetic: 21 us -> 0 us
  between operations: 13.9 us -> 0.66 us
    reduce_scatter x2 -> x0, waiting for transfers between devices: 690 us -> none  [the longest x1 581 us: per_device(): lax.psum_scatter(lax.dot_general(attended_all, grad_out, (((0,), (0,)), (...]
    psum x1 -> x0, blocking collectives: 159 us -> none  [per_device(): query_total, key_total = lax.psum((query_local, key_local), 'dp')]
    all_gather x2 -> x0, waiting for transfers between devices: 145 us -> none  [the longest x1 85.9 us: per_device(): lax.all_gather(out_weight, 'dp', axis=0, tiled=True)]
    pallas_call x0 -> x1, Pallas kernels: none -> 125 us  [per_device(): pl.pallas_call(kernel, out_shape=(tokens, tokens, tokens, jax.ShapeDtypeS...]
    dot_general x7 -> x0, matrix products: 61.7 us -> none  [the longest x1 12.6 us: per_device(): jnp.einsum('ihqk,iqhd->ikhd', grad_scores, query_hat, preferred_element_t...]
    reshape x7 -> x0, local copies, waits for them, and re-layouts: 23.9 us -> none  [the longest x2 8.23 us: per_device(): query_in.astype(jnp.float32).reshape(layout)]
    unnamed x29 -> x16, local copies, waits for them, and re-layouts: 20.7 us -> 7.75 us
    convert_element_type x4 -> x0, other arithmetic: 12.8 us -> none  [the longest x1 4.27 us: per_device(): norm_back(grad_qhat, query_norm, query_inverse, query_gain)]
  transfers between devices with their start and end apart: 4 -> 0, of which waited for: 4 -> 0; matrix products, arithmetic and copies ran while one was open for 12% -> 0% of each run, Pallas kernels for 0% -> 0%
where the time goes in v1:
time: 135 us; the launch traced here: 133 us
  Pallas kernels  125 us (93%)
  local copies, waits for them, and re-layouts  7.75 us (6%)
    pallas_call x1, Pallas kernels, per_device(): pl.pallas_call(kernel, out_shape=(tokens, tokens, tokens, jax.ShapeDtypeS...  125 us
    unnamed x16, local copies, waits for them, and re-layouts  7.75 us

profile of v1, /device:TPU:9, one launch (start us, length us, event | category | flops | bytes accessed | tf_op | source)
XLA Modules:
  0.0 133.1 jit_solution(15231936231582588831)
XLA Ops:
  0.6 124.7 %shard_map.118 = (bf16[1024,768]{1,0:T(8,128)(2,1)}, bf16[1024,768]{1,0:T(8,128)(2,1)}, bf16[1024,768]{1,0:T(8,128)(2,1)}, f32[48,768]{1,0:T(8,128)}, f32[6,128]{1,0:T(8,128)}, /*index=5*/f32[6,128]{1,0:T(8,128)}) custom-call(bf16[1024,768]{1,0:T(8,128)(2,1)} %q_hbm.1, bf16[1024,768]{1,0:T(8,128)(2,1)} %k_hbm.1, bf16[1024,768]{1,0:T(8,128)(2,1)} %v_hbm.1, ...), custom_call_target="tpu_custom_call" | custom-call | flops 12000000000 | bytes 12000000 | tf_op jit(solution)/shard_map/pallas_call | solution.py:478
  125.4 0.0 copy-start.1
  125.4 2.8 %copy.19 = bf16[1024,768]{1,0:T(8,128)(2,1)} copy(bf16[1024,768]{1,0:T(8,128)(2,1)} %get-tuple-element.12) | data formatting | bytes 3145728
  128.1 0.0 copy-done.1
  128.1 0.0 copy-start
  128.1 1.1 copy.20
  129.3 0.8 copy-done
  130.1 0.0 copy-start.2
  130.1 0.0 copy-start.4
  130.1 0.0 copy-start.3
  130.1 1.1 copy.21
  131.3 0.0 copy-done.2
  131.3 0.7 copy.22
  131.9 0.0 copy-done.4
  131.9 0.6 copy.23
  132.5 0.0 copy-done.3
  132.5 0.6 copy.24
Async XLA Ops:
  125.4 2.8 %copy-start.1 = (bf16[1024,768]{1,0:T(8,128)(2,1)S(1)}, bf16[1024,768]{1,0:T(8,128)(2,1)}, u32[]{:S(2)}) copy-start(bf16[1024,768]{1,0:T(8,128)(2,1)} %get-tuple-element.13) | copy-start | bytes 4718596
  128.1 2.0 %copy-start = (bf16[1024,768]{1,0:T(8,128)(2,1)S(1)}, bf16[1024,768]{1,0:T(8,128)(2,1)}, u32[]{:S(2)}) copy-start(bf16[1024,768]{1,0:T(8,128)(2,1)} %get-tuple-element.14) | copy-start | bytes 4718596
  130.1 1.2 copy-start.2
  130.1 1.8 %copy-start.4 = (f32[6,128]{1,0:T(8,128)S(1)}, f32[6,128]{1,0:T(8,128)}, u32[]{:S(2)}) copy-start(f32[6,128]{1,0:T(8,128)} %get-tuple-element.16) | copy-start | bytes 9220
  130.1 2.4 %copy-start.3 = (f32[6,128]{1,0:T(8,128)S(1)}, f32[6,128]{1,0:T(8,128)}, u32[]{:S(2)}) copy-start(f32[6,128]{1,0:T(8,128)} %get-tuple-element.17) | copy-start | bytes 9220

commit v2 on v1

v2 whole, which is shorter than its diff:
```python
import heapq
import itertools
import math

import jax
import jax.numpy as jnp
from jax import lax
from jax.experimental import pallas as pl
from jax.experimental.pallas import tpu as pltpu
from jax.sharding import PartitionSpec as P

PATCH = 256
HD = 128
EPS = 1e-06
F32 = jnp.float32
BF16 = jnp.bfloat16
MESH = pl.DeviceIdType.MESH
NZ, NX = 8, 4
FACTOR = 1.0 / math.sqrt(HD)

NN = (((1,), (0,)), ((), ()))
NT = (((1,), (1,)), ((), ()))
TN = (((0,), (0,)), ((), ()))


SIDES = (1, -1)
X_OUT, X_IN = (0, 1, -1, 2), (2, 1, -1, 0)
Z_OUT, Z_IN = (0, 1, -1, 2, -2, 3, -3, 4), (4, 3, -3, 2, -2, 1, -1, 0)
GATHER = ((("x", (0,)), ("z", X_OUT)), (("z", (0,)), ("x", Z_OUT)))
REDUCE = ((("z", X_IN), ("x", (0,))), (("x", Z_IN), ("z", (0,))))
HALF = {"z": NZ // 2, "x": NX // 2}


def keys_of(kind, table):
    for st in range(2):
        for ph in range(2):
            axis, offsets = table[st][ph]
            for o in offsets:
                for way in SIDES:
                    for step in range(HALF[axis]):
                        yield (kind, st, ph, o, way, step)


SLOT = {}
for kind, table in (("ag", GATHER), ("rs", REDUCE)):
    for number, key in enumerate(keys_of(kind, table)):
        SLOT[key] = number
COPIES = len(SLOT) // 2

FULL, LATENCY = 1.6, 1.5
COST = {"fw": 0.95, "wp": 1.6, "ga": 2.7, "bw": 1.1}


def make_plan():
    now = [0.0]
    free = {}
    heap = []
    ops = []
    done = set()
    tally = itertools.count()

    def arrive(key, at):
        heapq.heappush(heap, (at, next(tally), key))

    def send(key):
        kind, st, ph, o, way, step = key
        axis = (GATHER if kind == "ag" else REDUCE)[st][ph][0]
        halved = step == (HALF[axis] - 1 if kind == "ag" else 0)
        start = max(now[0], free.get((axis, way), 0.0))
        free[axis, way] = start + (FULL / 2 if halved else FULL)
        arrive(key, free[axis, way] + LATENCY)
        ops.append(("send", key))

    def gather_ready(st, o):
        for way in SIDES:
            send(("ag", st, 1, o, way, 0))

    forwards = [sum(1 for k in keys_of("ag", GATHER) if k[5] + 1 < HALF[GATHER[k[1]][k[2]][0]])]

    def try_reduce():
        if forwards[0] or now[0] < 0:
            return
        for st, needs in ((0, ("own", "core")), (1, ("near", "far"))):
            if ("start", st) not in done and all(("wp", n) in done for n in needs):
                done.add(("start", st))
                for o in REDUCE[st][0][1]:
                    for way in SIDES:
                        send(("rs", st, 0, o, way, 0))

    def try_second(st, way, step):
        half = HALF[REDUCE[st][1][0]]
        o = way * (half - step)
        if abs(o) == half:
            o = half
        axis = REDUCE[st][0][0]
        last = HALF[axis] - 1
        ready = all(("rs", st, 0, o, w, last) in done for w in SIDES)
        if ready and (step == 0 or ("rs", st, 1, 0, way, step - 1) in done):
            key = ("rs", st, 1, 0, way, step)
            if ("sent", key) not in done:
                done.add(("sent", key))
                send(key)

    def process(key):
        ops.append(("recv", key))
        done.add(key)
        now[0] += 0.05
        if key == ("wred",):
            for st in (1, 0):
                for way in SIDES:
                    send(("ag", st, 0, 0, way, 0))
                gather_ready(st, 0)
        elif key[0] == "gy":
            arrive(("gf", key[1]), now[0] + 2.5)
        elif key == ("gain", 0):
            arrive(("gain", 1), now[0] + 3.0)
        elif key[0] == "ag":
            _, st, ph, o, way, step = key
            half = HALF[GATHER[st][ph][0]]
            if step + 1 < half:
                forwards[0] -= 1
                send(("ag", st, ph, o, way, step + 1))
            if ph == 0:
                if step + 1 < half:
                    gather_ready(st, -way * (step + 1))
                elif ("ag", st, 0, 0, -way, step) in done:
                    gather_ready(st, half)
            try_reduce()
        elif key[0] == "rs":
            _, st, ph, o, way, step = key
            half = HALF[REDUCE[st][ph][0]]
            if ph == 0:
                if step + 1 < half:
                    send(("rs", st, 0, o, way, step + 1))
                else:
                    for w in SIDES:
                        for later in range(HALF[REDUCE[st][1][0]]):
                            try_second(st, w, later)
            else:
                if step + 1 < half:
                    try_second(st, way, step + 1)
            total = [k for k in keys_of("rs", REDUCE) if k[1] == st]
            if all(k in done for k in total):
                ops.append(("final", st))

    work = [("fw", i) for i in range(12)]
    work += [("wp", n) for n in ("own", "core", "near", "far")]
    for t in range(2):
        work += [("ga", t)] + [("bw", 6 * t + i) for i in range(6)]
    gathered = set(keys_of("ag", GATHER))

    def ready(unit):
        kind, n = unit
        if kind == "wp" and n == "core":
            return ("gc",) in done
        if kind == "wp" and n == "near":
            return ("gy", 3) in done
        if kind == "wp" and n == "far":
            return ("gf", 3) in done
        if kind == "ga":
            return gathered <= done and all(("gf", i) in done for i in range(4))
        return True

    arrive(("wred",), 6.3)
    arrive(("gc",), 8.0)
    for i in range(4):
        arrive(("gy", i), 8.4 * (i + 1) + 3.5)
    while heap or work:
        if heap and heap[0][0] <= now[0]:
            process(heapq.heappop(heap)[2])
        elif work and ready(work[0]):
            unit = work.pop(0)
            ops.append(unit)
            done.add(unit)
            now[0] += COST[unit[0]]
            try_reduce()
            if unit == ("bw", 11):
                ops.append(("gain", 0))
                arrive(("gain", 0), now[0] + 3.0)
        else:
            now[0] = max(now[0], heap[0][0])
    return ops, now[0]


PLAN = make_plan()[0]
POOL = 64
SENDS = [op[1] for op in PLAN if op[0] == "send"]
ORDER = {key: n for n, key in enumerate(SENDS)}


def dot(a, b, dims):
    return lax.dot_general(a, b, dims, preferred_element_type=F32)


def device(z, x, yh, yl, c):
    return {"dp": (z * NX + x) * 2 + yh, "mp": yl * 2 + c}


def kernel(
    q_hbm, k_hbm, v_hbm, g_hbm, w_hbm, qgain, kgain,
    gq_hbm, gk_hbm, gv_hbm, gw_hbm, qg_hbm, kg_hbm,
    qb, kb, vb, G, W7, P7, attT, qh, kh, probs, gatt,
    landing, fin, gacc, gbuf, gw_out, small_sem,
    ld_sem, own_sem, out_sem,
    wr_s, wr_r, gy_s, gy_r, gc_s, gc_r, gf_s, gf_r,
    ring_s, ag_r, rs_r, fin_s, fin_r, ga_s, ga_r,
):
    dp, mp = lax.axis_index("dp"), lax.axis_index("mp")
    z, x, yh = dp // 8, (dp // 2) % 4, dp % 2
    yl, c = mp // 2, mp % 2
    m_src, zl_src = z // 2, z % 2
    rem = lax.rem

    def bits(zz):
        r = rem(zz - 2 * mp + NZ, NZ)
        upper = (r >= 1) & (r <= 4)
        t = jnp.where(upper, r - 1, rem(NZ - r, NZ))
        return upper.astype(jnp.int32), t // 2, t % 2

    z_at = {o: rem(z + o + NZ, NZ) for o in range(-4, 5)}
    x_at = {o: rem(x + o + NX, NX) for o in range(-2, 3)}
    bits_at = {o: bits(z_at[o]) for o in range(-3, 5)}
    bits_at[-4] = bits_at[4]
    zl, yb, cb = bits_at[0]

    def to_plane(half):
        target = rem(z + (2 * zl_src - 1) * (yh * 2 + c) + NZ, NZ)
        return target, x, half, m_src // 2, m_src % 2

    def to_owner(s):
        return mp * 2 + zl, x, yb, s, cb

    def is_me(d):
        same = (d[0] == z) & (d[1] == x) & (d[2] == yh)
        return same & (d[3] == yl) & (d[4] == c)

    barrier = pltpu.get_barrier_semaphore()

    def greet(d):
        pl.semaphore_signal(barrier, inc=1, device_id=device(*d), device_id_type=MESH)

    j = x * 2 + yh
    for step in range(1, 8):
        greet((rem(z + step, 8), x, yh, yl, c))
        jj = rem(j + step, 8)
        greet((z, jj // 2, jj % 2, yl, c))
    greet((z, x, yh, 1 - yl, c))
    greet((z, x, yh, yl, 1 - c))
    count = jnp.int32(20)
    for d in (to_plane(0), to_plane(1), to_owner(0), to_owner(1)):
        mine = is_me(d)
        count = count - mine.astype(jnp.int32)
        pl.when(jnp.logical_not(mine))(lambda d=d: greet(d))

    def load(a, i):
        src, dst = ((q_hbm, qb), (k_hbm, kb), (v_hbm, vb))[a]
        rows = pl.ds(i * PATCH, PATCH)
        return pltpu.make_async_copy(src.at[rows], dst.at[rows], ld_sem.at[a, i])

    for i in range(4):
        for a in range(3):
            load(a, i).start()
    own_load = pltpu.make_async_copy(g_hbm, G.at[mp], own_sem)
    own_load.start()
    pl.semaphore_wait(barrier, count)

    def remote(src, dst, send, recv, d):
        return pltpu.make_async_remote_copy(
            src_ref=src, dst_ref=dst, send_sem=send, recv_sem=recv,
            device_id=device(*d), device_id_type=MESH,
        )

    def w_copy(half):
        return remote(w_hbm, W7.at[yl, c, zl_src, x, yh], wr_s.at[half], wr_r.at[yl], to_plane(half))

    for half in range(2):
        mine = is_me(to_plane(half))
        pl.when(jnp.logical_not(mine))(lambda half=half: w_copy(half).start())
        pl.when(mine)(
            lambda: pltpu.make_async_copy(
                w_hbm, W7.at[yl, c, zl_src, x, yh], wr_r.at[yl]
            ).start()
        )

    def w_arrive(s):
        here = W7.at[s, cb, zl, x, yb]
        pltpu.make_async_copy(here, here, wr_r.at[s]).wait()

    def g_rows(ref, i):
        return ref.at[pl.ds(i * PATCH, PATCH)]

    def gy(i, block):
        return remote(g_rows(g_hbm, i), g_rows(G.at[block], i), gy_s.at[i], gy_r.at[i], (z, x, yh, 1 - yl, c))

    def gc(i, block):
        return remote(g_rows(g_hbm, i), g_rows(G.at[block], i), gc_s.at[i], gc_r.at[i], (z, x, yh, yl, 1 - c))

    def gf(i, block):
        part = g_rows(G.at[block], i)
        return remote(part, part, gf_s.at[i], gf_r.at[i], (z, x, yh, yl, 1 - c))

    near = (1 - yl) * 2 + c
    core = yl * 2 + 1 - c
    far = (1 - yl) * 2 + 1 - c
    for i in range(4):
        gy(i, mp).start()
    for i in range(4):
        gc(i, mp).start()

    def g_forward(i):
        gy(i, near).wait_recv()
        gf(i, near).start()

    def side(st):
        return yl if st == 0 else 1 - yl

    def block(ref, st, axis, along, across):
        zo, xo = (along, across) if axis == "z" else (across, along)
        a, b, d = bits_at[zo]
        return ref.at[side(st), d, a, x_at[xo], b]

    def half_of(ref, which):
        return ref.at[:, pl.ds(which * 384, 384)]

    def neighbour(axis, way):
        return (z_at[way], x, yh, yl, c) if axis == "z" else (z, x_at[way], yh, yl, c)

    def ag_copy(key, back):
        _, st, ph, o, way, step = key
        axis = GATHER[st][ph][0]
        ref = block(W7, st, axis, -way * back, o)
        if step == HALF[axis] - 1:
            ref = half_of(ref, 0 if way > 0 else 1)
        return remote(ref, ref, ring_s.at[ORDER[key] % POOL], ag_r.at[SLOT[key]], neighbour(axis, way))

    def rs_refs(key, off):
        _, st, ph, o, way, step = key
        axis = REDUCE[st][ph][0]
        ref, dst = block(P7, st, axis, way * off, o), landing.at[SLOT[key]]
        if step == 0:
            k = 0 if way > 0 else 1
            ref, dst = half_of(ref, k), half_of(dst, k)
        return ref, dst

    def rs_copy(key, off):
        ref, dst = rs_refs(key, off)
        to = neighbour(REDUCE[key[1]][key[2]][0], key[4])
        return remote(ref, dst, ring_s.at[ORDER[key] % POOL], rs_r.at[SLOT[key]], to)

    def send_copy(key):
        if key[0] == "ag":
            return ag_copy(key, key[5])
        return rs_copy(key, HALF[REDUCE[key[1]][key[2]][0]] - key[5])

    def receive(key):
        if key[0] == "ag":
            ag_copy(key, key[5] + 1).wait_recv()
        else:
            off = HALF[REDUCE[key[1]][key[2]][0]] - 1 - key[5]
            rs_copy(key, off).wait_recv()
            ref, got = rs_refs(key, off)
            ref[...] = (ref[...].astype(F32) + got[...].astype(F32)).astype(BF16)

    def fin_copy(st):
        s = side(st)
        return remote(P7.at[s, cb, zl, x, yb], fin.at[yh], fin_s.at[st], fin_r.at[yh], to_owner(s))

    def final(st):
        s = side(st)
        mine = is_me(to_owner(s))
        pl.when(jnp.logical_not(mine))(lambda: fin_copy(st).start())
        pl.when(mine)(
            lambda: pltpu.make_async_copy(P7.at[s, cb, zl, x, yb], fin.at[yh], fin_r.at[yh]).start()
        )

    def normed(v):
        v = v.astype(F32)
        v = v - jnp.mean(v, axis=-1, keepdims=True)
        inverse = lax.rsqrt(jnp.mean(v * v, axis=-1, keepdims=True) + EPS)
        return v * inverse, inverse

    def place(it):
        rows = pl.ds(pl.multiple_of(it // 3 * PATCH, PATCH), PATCH)
        h = rem(it, 3) * 2
        return [(rows, pl.ds(pl.multiple_of((h + n) * HD, HD), HD), pl.ds(h + n, 1), n) for n in range(2)]

    def forward(it):
        units = place(it)
        qs = [qb[rows, cols] for rows, cols, _, _ in units]
        ks = [kb[rows, cols] for rows, cols, _, _ in units]
        vs = [vb[rows, cols] for rows, cols, _, _ in units]
        a_hat = [(normed(q)[0] * qgain[u[2], :]).astype(BF16) for q, u in zip(qs, units)]
        b_hat = [(normed(k)[0] * kgain[u[2], :]).astype(BF16) for k, u in zip(ks, units)]
        scores = [dot(b, a, NT) * FACTOR for a, b in zip(a_hat, b_hat)]
        expo = [jnp.exp(s - jnp.max(s, axis=0, keepdims=True)) for s in scores]
        ps = [e * (1.0 / jnp.sum(e, axis=0, keepdims=True)) for e in expo]
        att = [dot(v, p.astype(BF16), TN).astype(BF16) for v, p in zip(vs, ps)]
        for a, b, p, t, (rows, cols, _, n) in zip(a_hat, b_hat, ps, att, units):
            qh[rows, cols] = a
            kh[rows, cols] = b
            probs[it * 2 + n] = p
            attT[cols, rows] = t

    def back(grad, normal, inverse, gain):
        u = grad * gain
        spread = jnp.mean(u * normal, axis=-1, keepdims=True)
        return ((u - jnp.mean(u, axis=-1, keepdims=True) - normal * spread) * inverse).astype(BF16)

    def backward(it):
        units = place(it)
        gas = [gatt[rows, cols] for rows, cols, _, _ in units]
        vs = [vb[rows, cols] for rows, cols, _, _ in units]
        qhs = [qh[rows, cols] for rows, cols, _, _ in units]
        khs = [kh[rows, cols] for rows, cols, _, _ in units]
        qs = [normed(qb[rows, cols]) for rows, cols, _, _ in units]
        ks = [normed(kb[rows, cols]) for rows, cols, _, _ in units]
        ps = [probs[it * 2 + n] for n in range(2)]
        gps = [dot(v, ga, NT) for v, ga in zip(vs, gas)]
        gvs = [dot(p.astype(BF16), ga, NN).astype(BF16) for p, ga in zip(ps, gas)]
        inner = [jnp.sum(p * gp, axis=0, keepdims=True) for p, gp in zip(ps, gps)]
        gss = [(p * (gp - n) * FACTOR).astype(BF16) for p, gp, n in zip(ps, gps, inner)]
        gks = [dot(g, a, NN) for g, a in zip(gss, qhs)]
        gqs = [dot(g, b, TN) for g, b in zip(gss, khs)]
        qsum = [jnp.sum(g * a, axis=0, keepdims=True) for g, (a, _) in zip(gqs, qs)]
        ksum = [jnp.sum(g * b, axis=0, keepdims=True) for g, (b, _) in zip(gks, ks)]
        qout = [back(g, a, i, qgain[u[2], :]) for g, (a, i), u in zip(gqs, qs, units)]
        kout = [back(g, b, i, kgain[u[2], :]) for g, (b, i), u in zip(gks, ks, units)]
        for (rows, cols, _, n), gv, gq, gk in zip(units, gvs, qout, kout):
            vb[rows, cols] = gv
            qb[rows, cols] = gq
            kb[rows, cols] = gk
        h = rem(it, 3) * 2
        for n in range(2):
            gacc[0, pl.ds(h + n, 1), :] += qsum[n]
            gacc[0, pl.ds(8 + h + n, 1), :] += ksum[n]

    def weight_partial(block):
        s, d = block // 2, block % 2

        def body(t, carry):
            rows = pl.ds(pl.multiple_of(t * 384, 128), 384)
            part = dot(attT[rows, :], G[block], NN).astype(BF16)
            P7[s, d, t] = part.reshape(4, 2, 48, 768)
            return carry

        lax.fori_loop(0, 2, body, 0)

    def attended_grad(t):
        rows = pl.ds(pl.multiple_of(t * 512, 512), 512)
        total = None
        for block in range(4):
            w = W7[block // 2, block % 2].reshape(768, 768)
            part = dot(G[block, rows, :], w, NT)
            total = part if total is None else total + part
        gatt[rows, :] = total.astype(BF16)

    def store(a, i):
        src, dst = ((qb, gq_hbm), (kb, gk_hbm), (vb, gv_hbm))[a]
        rows = pl.ds(i * PATCH, PATCH)
        return pltpu.make_async_copy(src.at[rows], dst.at[rows], out_sem.at[a, i])

    def gain_copy(ph, step):
        if ph == 0:
            jj = rem(j + step, 8)
            d = (z, jj // 2, jj % 2, yl, c)
        else:
            d = (rem(z + step, 8), x, yh, yl, c)
        return remote(
            gacc.at[ph], gbuf.at[ph, step - 1], ga_s.at[ph], ga_r.at[ph], d
        )

    def gain_send(ph):
        for step in range(1, 8):
            gain_copy(ph, step).start()

    def gain_out(a):
        dst = (qg_hbm, kg_hbm)[a]
        return pltpu.make_async_copy(gacc.at[2, pl.ds(a * 8, 8)], dst, small_sem.at[a])

    def gain_wait(ph, sem):
        pltpu.make_async_copy(gbuf.at[ph], gbuf.at[ph], sem.at[ph]).wait()

    def gain_sum(ph):
        gain_wait(ph, ga_r)
        total = gacc[ph]
        for step in range(1, 8):
            total = total + gbuf[ph, step - 1]
        return total

    def event(op):
        kind, what = op
        if kind == "send":
            if ORDER[what] >= POOL:
                send_copy(SENDS[ORDER[what] - POOL]).wait_send()
            send_copy(what).start()
        elif kind == "final":
            final(what)
        elif kind == "gain":
            gain_send(0)
        elif kind == "wp":
            if what == "own":
                own_load.wait()
            weight_partial({"own": mp, "core": core, "near": near, "far": far}[what])
        elif kind == "ga":
            attended_grad(what)
        elif what[0] == "wred":
            for s in range(2):
                w_arrive(s)
        elif what[0] == "gc":
            for i in range(4):
                gc(i, core).wait_recv()
        elif what[0] == "gy":
            g_forward(what[1])
        elif what[0] == "gf":
            gf(what[1], far).wait_recv()
        elif what[0] == "gain":
            total = gain_sum(what[1])
            if what[1] == 0:
                gacc[1] = total
                gain_send(1)
            else:
                gacc[2] = total
                gain_out(0).start()
                gain_out(1).start()
        else:
            receive(what)

    at = {op: n for n, op in enumerate(PLAN) if op[0] in ("fw", "bw")}
    between = {}
    for name in ("fw", "bw"):
        for i in range(12):
            end = at.get((name, i + 1), len(PLAN))
            between[name, i] = PLAN[at[name, i] + 1 : end] if i < 11 else []

    def first_body(it, carry):
        for i in range(4):
            @pl.when(it == i * 3)
            def _():
                for a in range(3):
                    load(a, i).wait()
        forward(it)
        for i in range(11):
            if between["fw", i]:
                @pl.when(it == i)
                def _():
                    for op in between["fw", i]:
                        event(op)
        return carry

    def second_body(it, carry):
        backward(it)
        for i in range(4):
            @pl.when(it == i * 3 + 2)
            def _():
                for a in range(3):
                    store(a, i).start()
        for i in range(11):
            if between["bw", i]:
                @pl.when(it == i)
                def _():
                    for op in between["bw", i]:
                        event(op)
        return carry

    gacc[...] = jnp.zeros_like(gacc)
    for op in PLAN[: at["fw", 0]]:
        event(op)
    lax.fori_loop(0, 12, first_body, 0)
    for op in PLAN[at["fw", 11] + 1 : at["bw", 0]]:
        event(op)
    lax.fori_loop(0, 12, second_body, 0)
    for op in PLAN[at["bw", 11] + 1 :]:
        event(op)

    for half in range(2):
        pl.when(jnp.logical_not(is_me(to_plane(half))))(lambda half=half: w_copy(half).wait_send())
    for i in range(4):
        gy(i, mp).wait_send()
        gc(i, mp).wait_send()
        gf(i, near).wait_send()
    for key in SENDS[-POOL:]:
        send_copy(key).wait_send()
    for ph in range(2):
        gain_wait(ph, ga_s)
    for half in range(2):
        pltpu.make_async_copy(fin.at[half], fin.at[half], fin_r.at[half]).wait()
    for st in range(2):
        pl.when(jnp.logical_not(is_me(to_owner(side(st)))))(lambda st=st: fin_copy(st).wait_send())
    gw_out[...] = fin[0].astype(F32) + fin[1].astype(F32)
    last = pltpu.make_async_copy(gw_out, gw_hbm, small_sem.at[2])
    last.start()
    for i in range(4):
        for a in range(3):
            store(a, i).wait()
    gain_out(0).wait()
    gain_out(1).wait()
    last.wait()


def hand_on(*refs):
    ins, outs, held, load_sem, store_sem = refs[:6], refs[6:12], refs[12:18], refs[18], refs[19]
    parts = []
    for a in range(6):
        pieces = 4 if a < 3 else 1
        rows = outs[a].shape[0] // pieces
        parts += [(a, pl.ds(i * rows, rows)) for i in range(pieces)]
    loads = [
        pltpu.make_async_copy(ins[a].at[part], held[a].at[part], load_sem.at[n])
        for n, (a, part) in enumerate(parts)
    ]
    stores = [
        pltpu.make_async_copy(held[a].at[part], outs[a].at[part], store_sem.at[n])
        for n, (a, part) in enumerate(parts)
    ]
    for load in loads:
        load.start()
    for load, store in zip(loads, stores):
        load.wait()
        store.start()
    for store in stores:
        store.wait()


def per_device(query_in, key_in, value_in, grad_out, out_weight, query_gain, key_gain):
    vmem = pl.BlockSpec(memory_space=pltpu.VMEM)
    anywhere = pl.BlockSpec(memory_space=pl.ANY)
    tokens = jax.ShapeDtypeStruct((1024, 768), BF16)
    dma = pltpu.SemaphoreType.DMA
    act = pltpu.VMEM((1024, 768), BF16)
    big = pltpu.VMEM((2, 2, 2, 4, 2, 48, 768), BF16)
    results = pl.pallas_call(
        kernel,
        out_shape=(
            tokens, tokens, tokens,
            jax.ShapeDtypeStruct((48, 768), F32),
            jax.ShapeDtypeStruct((8, 128), F32),
            jax.ShapeDtypeStruct((8, 128), F32),
        ),
        in_specs=[anywhere] * 5 + [vmem] * 2,
        out_specs=(anywhere,) * 6,
        scratch_shapes=[
            act, act, act,
            pltpu.VMEM((4, 1024, 768), BF16),
            big, big,
            pltpu.VMEM((768, 1024), BF16),
            act, act,
            pltpu.VMEM((24, 256, 256), F32),
            act,
            pltpu.VMEM((COPIES, 48, 768), BF16),
            pltpu.VMEM((2, 48, 768), BF16),
            pltpu.VMEM((3, 16, 128), F32),
            pltpu.VMEM((2, 7, 16, 128), F32),
            pltpu.VMEM((48, 768), F32),
            dma((3,)),
            dma((3, 4)), dma, dma((3, 4)),
            dma((2,)), dma((2,)), dma((4,)), dma((4,)), dma((4,)), dma((4,)), dma((4,)), dma((4,)),
            dma((POOL,)), dma((COPIES,)), dma((COPIES,)),
            dma((2,)), dma((2,)), dma((2,)), dma((2,)),
        ],
        compiler_params=pltpu.CompilerParams(
            collective_id=0, has_side_effects=True, vmem_limit_bytes=60 * 2**20
        ),
        cost_estimate=pl.CostEstimate(flops=12 * 10**9, bytes_accessed=12 * 10**6, transcendentals=1600000),
    )(query_in, key_in, value_in, grad_out, out_weight, query_gain, key_gain)
    return pl.pallas_call(
        hand_on,
        out_shape=(
            tokens, tokens, tokens,
            jax.ShapeDtypeStruct((48, 768), F32),
            jax.ShapeDtypeStruct((6, 128), F32),
            jax.ShapeDtypeStruct((6, 128), F32),
        ),
        in_specs=[anywhere] * 6,
        out_specs=(anywhere,) * 6,
        scratch_shapes=[
            act, act, act,
            pltpu.VMEM((48, 768), F32), pltpu.VMEM((6, 128), F32), pltpu.VMEM((6, 128), F32),
            dma((15,)), dma((15,)),
        ],
    )(*results)


def solution(mesh):
    rows = P("dp", "mp")
    heads = P("mp", None)
    return jax.shard_map(
        per_device,
        mesh=mesh,
        in_specs=(rows, rows, rows, rows, rows, heads, heads),
        out_specs=(rows, rows, rows, rows, heads, heads),
        check_vma=False,
    )
```

time: 135 us -> 101 us (0.75); the launches traced: 133 us -> 101 us
  Pallas kernels: 125 us -> 100 us
  local copies, waits for them, and re-layouts: 7.75 us -> 0 us
    pallas_call x1, Pallas kernels: 125 us -> 95.7 us  [per_device(): pl.pallas_call(kernel, out_shape=(tokens, tokens, tokens, jax.ShapeDtypeS...]
    unnamed x16 -> x0, local copies, waits for them, and re-layouts: 7.75 us -> none
    pallas_call x0 -> x1, Pallas kernels: none -> 4.37 us  [per_device(): pl.pallas_call(hand_on, out_shape=(tokens, tokens, tokens, jax.ShapeDtype...]
where the time goes in v2:
time: 101 us
  Pallas kernels  100 us (99%)
    pallas_call x1, Pallas kernels, per_device(): pl.pallas_call(kernel, out_shape=(tokens, tokens, tokens, jax.ShapeDtypeS...  95.7 us
    pallas_call x1, Pallas kernels, per_device(): pl.pallas_call(hand_on, out_shape=(tokens, tokens, tokens, jax.ShapeDtype...  4.37 us

profile of v2, /device:TPU:9, one launch (start us, length us, event | category | flops | bytes accessed | tf_op | source)
XLA Modules:
  0.0 100.7 jit_solution(5733869774691513076)
XLA Ops:
  0.6 95.7 %shard_map.118 = (bf16[1024,768]{1,0:T(8,128)(2,1)}, bf16[1024,768]{1,0:T(8,128)(2,1)}, bf16[1024,768]{1,0:T(8,128)(2,1)}, f32[48,768]{1,0:T(8,128)}, f32[8,128]{1,0:T(8,128)}, /*index=5*/f32[8,128]{1,0:T(8,128)}) custom-call(bf16[1024,768]{1,0:T(8,128)(2,1)} %q_hbm.1, bf16[1024,768]{1,0:T(8,128)(2,1)} %k_hbm.1, bf16[1024,768]{1,0:T(8,128)(2,1)} %v_hbm.1, ...), custom_call_target="tpu_custom_call" | custom-call | flops 12000000000 | bytes 12000000 | tf_op jit(solution)/shard_map/pallas_call | solution.py:631
  96.3 4.4 %shard_map.119 = (bf16[1024,768]{1,0:T(8,128)(2,1)}, bf16[1024,768]{1,0:T(8,128)(2,1)}, bf16[1024,768]{1,0:T(8,128)(2,1)}, f32[48,768]{1,0:T(8,128)}, f32[6,128]{1,0:T(8,128)}, /*index=5*/f32[6,128]{1,0:T(8,128)}) custom-call(bf16[1024,768]{1,0:T(8,128)(2,1)} %get-tuple-element.12.refs_0_, bf16[1024,768]{1,0:T(8,128)(2,1)} %get-tuple-element.13.refs_1_, ...), custom_call_target="tpu_custom_call" | custom-call | tf_op jit(solution)/shard_map/pallas_call | solution.py:665

commit v3 on v2

--- a/solution.py
+++ b/solution.py
@@ -26,13 +26,15 @@
 SIDES = (1, -1)
 X_OUT, X_IN = (0, 1, -1, 2), (2, 1, -1, 0)
 Z_OUT, Z_IN = (0, 1, -1, 2, -2, 3, -3, 4), (4, 3, -3, 2, -2, 1, -1, 0)
-GATHER = ((("x", (0,)), ("z", X_OUT)), (("z", (0,)), ("x", Z_OUT)))
+Z_FIRST = (("z", (0,)), ("x", Z_OUT))
+GATHER = ((("x", (0,)), ("z", X_OUT)), Z_FIRST, Z_FIRST)
+COLUMNS = ((0, 512), (0, 768), (512, 256))
 REDUCE = ((("z", X_IN), ("x", (0,))), (("x", Z_IN), ("z", (0,))))
 HALF = {"z": NZ // 2, "x": NX // 2}
 
 
 def keys_of(kind, table):
-    for st in range(2):
+    for st in range(len(table)):
         for ph in range(2):
             axis, offsets = table[st][ph]
             for o in offsets:
@@ -45,10 +47,12 @@
 for kind, table in (("ag", GATHER), ("rs", REDUCE)):
     for number, key in enumerate(keys_of(kind, table)):
         SLOT[key] = number
-COPIES = len(SLOT) // 2
-
+GATHERS = sum(1 for key in SLOT if key[0] == "ag")
+REDUCES = len(SLOT) - GATHERS
+
+HOLD = {}
 FULL, LATENCY = 1.6, 1.5
-COST = {"fw": 0.95, "wp": 1.6, "ga": 2.7, "bw": 1.1}
+COST = {"fw": 0.95, "wp": 1.6, "wa": 1.4, "gb": 1.45, "ga": 1.45, "bw": 1.1}
 
 
 def make_plan():
@@ -57,6 +61,7 @@
     heap = []
     ops = []
     done = set()
+    finish = [0.0]
     tally = itertools.count()
 
     def arrive(key, at):
@@ -67,7 +72,8 @@
         axis = (GATHER if kind == "ag" else REDUCE)[st][ph][0]
         halved = step == (HALF[axis] - 1 if kind == "ag" else 0)
         start = max(now[0], free.get((axis, way), 0.0))
-        free[axis, way] = start + (FULL / 2 if halved else FULL)
+        share = COLUMNS[st][1] / 768 if kind == "ag" else 1.0
+        free[axis, way] = start + FULL * share * (0.5 if halved else 1.0)
         arrive(key, free[axis, way] + LATENCY)
         ops.append(("send", key))
 
@@ -75,17 +81,16 @@
         for way in SIDES:
             send(("ag", st, 1, o, way, 0))
 
-    forwards = [sum(1 for k in keys_of("ag", GATHER) if k[5] + 1 < HALF[GATHER[k[1]][k[2]][0]])]
+    feeders = {k for k in keys_of("ag", GATHER) if k[1] > 0 and k[2] == 0}
 
     def try_reduce():
-        if forwards[0] or now[0] < 0:
+        if not feeders <= done:
             return
         for st, needs in ((0, ("own", "core")), (1, ("near", "far"))):
             if ("start", st) not in done and all(("wp", n) in done for n in needs):
                 done.add(("start", st))
                 for o in REDUCE[st][0][1]:
-                    for way in SIDES:
-                        send(("rs", st, 0, o, way, 0))
+                    arrive(("go", st, o), now[0] + HOLD.get((st, o), 0.0))
 
     def try_second(st, way, step):
         half = HALF[REDUCE[st][1][0]]
@@ -102,23 +107,26 @@
                 send(key)
 
     def process(key):
+        if key[0] == "go":
+            for way in SIDES:
+                send(("rs", key[1], 0, key[2], way, 0))
+            return
         ops.append(("recv", key))
         done.add(key)
         now[0] += 0.05
         if key == ("wred",):
-            for st in (1, 0):
+            for st in (1, 2, 0):
                 for way in SIDES:
                     send(("ag", st, 0, 0, way, 0))
                 gather_ready(st, 0)
         elif key[0] == "gy":
             arrive(("gf", key[1]), now[0] + 2.5)
         elif key == ("gain", 0):
-            arrive(("gain", 1), now[0] + 3.0)
+            arrive(("gain", 1), now[0] + 6.0)
         elif key[0] == "ag":
             _, st, ph, o, way, step = key
             half = HALF[GATHER[st][ph][0]]
             if step + 1 < half:
-                forwards[0] -= 1
                 send(("ag", st, ph, o, way, step + 1))
             if ph == 0:
                 if step + 1 < half:
@@ -142,23 +150,29 @@
             total = [k for k in keys_of("rs", REDUCE) if k[1] == st]
             if all(k in done for k in total):
                 ops.append(("final", st))
+                finish[0] = max(finish[0], now[0] + 4.0)
 
     work = [("fw", i) for i in range(12)]
-    work += [("wp", n) for n in ("own", "core", "near", "far")]
+    work += [("wp", "own"), ("wp", "core"), ("wa", "near"), ("wa", "far"), ("wp", "near"), ("wp", "far")]
     for t in range(2):
-        work += [("ga", t)] + [("bw", 6 * t + i) for i in range(6)]
-    gathered = set(keys_of("ag", GATHER))
+        work += [("gb", t), ("ga", t)] + [("bw", 6 * t + i) for i in range(6)]
+    gathered = [{k for k in keys_of("ag", GATHER) if k[1] == st} for st in range(3)]
 
     def ready(unit):
         kind, n = unit
-        if kind == "wp" and n == "core":
-            return ("gc",) in done
-        if kind == "wp" and n == "near":
-            return ("gy", 3) in done
-        if kind == "wp" and n == "far":
-            return ("gf", 3) in done
+        if kind in ("wp", "wa"):
+            needs = {
+                ("wp", "own"): [], ("wp", "core"): [("gc",)],
+                ("wa", "near"): [("gy", 2)], ("wa", "far"): [("gf", 2)],
+                ("wp", "near"): [("gy", 3), ("wa", "near")], ("wp", "far"): [("gf", 3), ("wa", "far")],
+            }[unit]
+            return ("fw", 11) in done and all(need in done for need in needs)
+        if kind == "gb":
+            return gathered[1] <= done and ("gf", 2 * n + 1) in done
         if kind == "ga":
-            return gathered <= done and all(("gf", i) in done for i in range(4))
+            return gathered[0] | gathered[2] <= done and ("gb", n) in done and ("gc",) in done and ("wp", "own") in done
+        if kind == "bw":
+            return ("ga", n // 6) in done and (n == 0 or ("bw", n - 1) in done)
         return True
 
     arrive(("wred",), 6.3)
@@ -168,22 +182,23 @@
     while heap or work:
         if heap and heap[0][0] <= now[0]:
             process(heapq.heappop(heap)[2])
-        elif work and ready(work[0]):
-            unit = work.pop(0)
+        elif any(ready(unit) for unit in work):
+            unit = next(unit for unit in work if ready(unit))
+            work.remove(unit)
             ops.append(unit)
             done.add(unit)
             now[0] += COST[unit[0]]
             try_reduce()
             if unit == ("bw", 11):
                 ops.append(("gain", 0))
-                arrive(("gain", 0), now[0] + 3.0)
+                arrive(("gain", 0), now[0] + 3.5)
         else:
             now[0] = max(now[0], heap[0][0])
-    return ops, now[0]
+    return ops, max(now[0], finish[0])
 
 
 PLAN = make_plan()[0]
-POOL = 64
+POOL = 48
 SENDS = [op[1] for op in PLAN if op[0] == "send"]
 ORDER = {key: n for n, key in enumerate(SENDS)}
 
@@ -200,7 +215,7 @@
     q_hbm, k_hbm, v_hbm, g_hbm, w_hbm, qgain, kgain,
     gq_hbm, gk_hbm, gv_hbm, gw_hbm, qg_hbm, kg_hbm,
     qb, kb, vb, G, W7, P7, attT, qh, kh, probs, gatt,
-    landing, fin, gacc, gbuf, gw_out, small_sem,
+    landing, fin, gacc, gbuf, gw_out, wacc, ggacc, qn, kn, inv, small_sem,
     ld_sem, own_sem, out_sem,
     wr_s, wr_r, gy_s, gy_r, gc_s, gc_r, gf_s, gf_r,
     ring_s, ag_r, rs_r, fin_s, fin_r, ga_s, ga_r,
@@ -312,7 +327,7 @@
         gf(i, near).start()
 
     def side(st):
-        return yl if st == 0 else 1 - yl
+        return 1 - yl if st == 1 else yl
 
     def block(ref, st, axis, along, across):
         zo, xo = (along, across) if axis == "z" else (across, along)
@@ -328,9 +343,11 @@
     def ag_copy(key, back):
         _, st, ph, o, way, step = key
         axis = GATHER[st][ph][0]
-        ref = block(W7, st, axis, -way * back, o)
+        first, width = COLUMNS[st]
         if step == HALF[axis] - 1:
-            ref = half_of(ref, 0 if way > 0 else 1)
+            cut = width // 2
+            first, width = (first, cut) if way > 0 else (first + cut, width - cut)
+        ref = block(W7, st, axis, -way * back, o).at[:, pl.ds(first, width)]
         return remote(ref, ref, ring_s.at[ORDER[key] % POOL], ag_r.at[SLOT[key]], neighbour(axis, way))
 
     def rs_refs(key, off):
@@ -359,7 +376,7 @@
             off = HALF[REDUCE[key[1]][key[2]][0]] - 1 - key[5]
             rs_copy(key, off).wait_recv()
             ref, got = rs_refs(key, off)
-            ref[...] = (ref[...].astype(F32) + got[...].astype(F32)).astype(BF16)
+            ref[...] = ref[...] + got[...]
 
     def fin_copy(st):
         s = side(st)
@@ -389,8 +406,10 @@
         qs = [qb[rows, cols] for rows, cols, _, _ in units]
         ks = [kb[rows, cols] for rows, cols, _, _ in units]
         vs = [vb[rows, cols] for rows, cols, _, _ in units]
-        a_hat = [(normed(q)[0] * qgain[u[2], :]).astype(BF16) for q, u in zip(qs, units)]
-        b_hat = [(normed(k)[0] * kgain[u[2], :]).astype(BF16) for k, u in zip(ks, units)]
+        qs = [normed(q) for q in qs]
+        ks = [normed(k) for k in ks]
+        a_hat = [(a * qgain[u[2], :]).astype(BF16) for (a, _), u in zip(qs, units)]
+        b_hat = [(b * kgain[u[2], :]).astype(BF16) for (b, _), u in zip(ks, units)]
         scores = [dot(b, a, NT) * FACTOR for a, b in zip(a_hat, b_hat)]
         expo = [jnp.exp(s - jnp.max(s, axis=0, keepdims=True)) for s in scores]
         ps = [e * (1.0 / jnp.sum(e, axis=0, keepdims=True)) for e in expo]
@@ -400,6 +419,8 @@
             kh[rows, cols] = b
             probs[it * 2 + n] = p
             attT[cols, rows] = t
+            qn[rows, cols], kn[rows, cols] = qs[n][0], ks[n][0]
+            inv[it * 2 + n, :, 0:1], inv[it * 2 + n, :, 1:2] = qs[n][1], ks[n][1]
 
     def back(grad, normal, inverse, gain):
         u = grad * gain
@@ -412,8 +433,8 @@
         vs = [vb[rows, cols] for rows, cols, _, _ in units]
         qhs = [qh[rows, cols] for rows, cols, _, _ in units]
         khs = [kh[rows, cols] for rows, cols, _, _ in units]
-        qs = [normed(qb[rows, cols]) for rows, cols, _, _ in units]
-        ks = [normed(kb[rows, cols]) for rows, cols, _, _ in units]
+        qs = [(qn[rows, cols], inv[it * 2 + n, :, 0:1]) for rows, cols, _, n in units]
+        ks = [(kn[rows, cols], inv[it * 2 + n, :, 1:2]) for rows, cols, _, n in units]
         ps = [probs[it * 2 + n] for n in range(2)]
         gps = [dot(v, ga, NT) for v, ga in zip(vs, gas)]
         gvs = [dot(p.astype(BF16), ga, NN).astype(BF16) for p, ga in zip(ps, gas)]
@@ -435,24 +456,43 @@
             gacc[0, pl.ds(8 + h + n, 1), :] += ksum[n]
 
     def weight_partial(block):
-        s, d = block // 2, block % 2
-
         def body(t, carry):
             rows = pl.ds(pl.multiple_of(t * 384, 128), 384)
             part = dot(attT[rows, :], G[block], NN).astype(BF16)
-            P7[s, d, t] = part.reshape(4, 2, 48, 768)
+            P7[block // 2, block % 2, t] = part.reshape(4, 2, 48, 768)
             return carry
 
         lax.fori_loop(0, 2, body, 0)
 
-    def attended_grad(t):
+    def weight_begin(n, block):
+        def body(t, carry):
+            rows = pl.ds(pl.multiple_of(t * 384, 128), 384)
+            wacc[n, rows, :] = dot(attT[rows, 0:768], G[block, 0:768, :], NN)
+            return carry
+
+        lax.fori_loop(0, 2, body, 0)
+
+    def weight_end(n, block):
+        def body(t, carry):
+            rows = pl.ds(pl.multiple_of(t * 384, 128), 384)
+            part = wacc[n, rows, :] + dot(attT[rows, 768:1024], G[block, 768:1024, :], NN)
+            P7[block // 2, block % 2, t] = part.astype(BF16).reshape(4, 2, 48, 768)
+            return carry
+
+        lax.fori_loop(0, 2, body, 0)
+
+    def attended_part(t, s):
         rows = pl.ds(pl.multiple_of(t * 512, 512), 512)
-        total = None
-        for block in range(4):
-            w = W7[block // 2, block % 2].reshape(768, 768)
-            part = dot(G[block, rows, :], w, NT)
-            total = part if total is None else total + part
-        gatt[rows, :] = total.astype(BF16)
+        parts = [dot(G[s * 2 + n, rows, :], W7[s, n].reshape(768, 768), NT) for n in range(2)]
+        return rows, parts[0] + parts[1]
+
+    def attended_begin(t):
+        rows, part = attended_part(t, 1 - yl)
+        ggacc[rows, :] = part
+
+    def attended_end(t):
+        rows, part = attended_part(t, yl)
+        gatt[rows, :] = (ggacc[rows, :] + part).astype(BF16)
 
     def store(a, i):
         src, dst = ((qb, gq_hbm), (kb, gk_hbm), (vb, gv_hbm))[a]
@@ -500,9 +540,16 @@
         elif kind == "wp":
             if what == "own":
                 own_load.wait()
-            weight_partial({"own": mp, "core": core, "near": near, "far": far}[what])
+            if what in ("own", "core"):
+                weight_partial(mp if what == "own" else core)
+            else:
+                weight_end(*((0, near) if what == "near" else (1, far)))
+        elif kind == "wa":
+            weight_begin(*((0, near) if what == "near" else (1, far)))
+        elif kind == "gb":
+            attended_begin(what)
         elif kind == "ga":
-            attended_grad(what)
+            attended_end(what)
         elif what[0] == "wred":
             for s in range(2):
                 w_arrive(s)
@@ -601,7 +648,7 @@
     ins, outs, held, load_sem, store_sem = refs[:6], refs[6:12], refs[12:18], refs[18], refs[19]
     parts = []
     for a in range(6):
-        pieces = 4 if a < 3 else 1
+        pieces = 2 if a < 3 else 1
         rows = outs[a].shape[0] // pieces
         parts += [(a, pl.ds(i * rows, rows)) for i in range(pieces)]
     loads = [
@@ -646,15 +693,19 @@
             act, act,
             pltpu.VMEM((24, 256, 256), F32),
             act,
-            pltpu.VMEM((COPIES, 48, 768), BF16),
+            pltpu.VMEM((REDUCES, 48, 768), BF16),
             pltpu.VMEM((2, 48, 768), BF16),
             pltpu.VMEM((3, 16, 128), F32),
             pltpu.VMEM((2, 7, 16, 128), F32),
             pltpu.VMEM((48, 768), F32),
+            pltpu.VMEM((2, 768, 768), F32),
+            pltpu.VMEM((1024, 768), F32),
+            pltpu.VMEM((1024, 768), F32), pltpu.VMEM((1024, 768), F32),
+            pltpu.VMEM((24, 256, 2), F32),
             dma((3,)),
             dma((3, 4)), dma, dma((3, 4)),
             dma((2,)), dma((2,)), dma((4,)), dma((4,)), dma((4,)), dma((4,)), dma((4,)), dma((4,)),
-            dma((POOL,)), dma((COPIES,)), dma((COPIES,)),
+            dma((POOL,)), dma((GATHERS,)), dma((REDUCES,)),
             dma((2,)), dma((2,)), dma((2,)), dma((2,)),
         ],
         compiler_params=pltpu.CompilerParams(

time: 101 us -> 96.4 us (0.954)
  Pallas kernels: 100 us -> 94.7 us
    pallas_call x1, Pallas kernels: 95.7 us -> 90.5 us  [per_device(): pl.pallas_call(kernel, out_shape=(tokens, tokens, tokens, jax.ShapeDtypeS...]
where the time goes in v3:
time: 96.4 us; the launch traced here: 95.3 us
  Pallas kernels  94.7 us (98%)
    pallas_call x1, Pallas kernels, per_device(): pl.pallas_call(kernel, out_shape=(tokens, tokens, tokens, jax.ShapeDtypeS...  90.5 us
    pallas_call x1, Pallas kernels, per_device(): pl.pallas_call(hand_on, out_shape=(tokens, tokens, tokens, jax.ShapeDtype...  4.17 us

profile of v3, /device:TPU:9, one launch (start us, length us, event | category | flops | bytes accessed | tf_op | source)
XLA Modules:
  0.0 95.3 jit_solution(11643445616226399950)
XLA Ops:
  0.6 90.5 %shard_map.118 = (bf16[1024,768]{1,0:T(8,128)(2,1)}, bf16[1024,768]{1,0:T(8,128)(2,1)}, bf16[1024,768]{1,0:T(8,128)(2,1)}, f32[48,768]{1,0:T(8,128)}, f32[8,128]{1,0:T(8,128)}, /*index=5*/f32[8,128]{1,0:T(8,128)}) custom-call(bf16[1024,768]{1,0:T(8,128)(2,1)} %q_hbm.1, bf16[1024,768]{1,0:T(8,128)(2,1)} %k_hbm.1, bf16[1024,768]{1,0:T(8,128)(2,1)} %v_hbm.1, ...), custom_call_target="tpu_custom_call" | custom-call | flops 12000000000 | bytes 12000000 | tf_op jit(solution)/shard_map/pallas_call | solution.py:678
  91.2 4.2 %shard_map.119 = (bf16[1024,768]{1,0:T(8,128)(2,1)}, bf16[1024,768]{1,0:T(8,128)(2,1)}, bf16[1024,768]{1,0:T(8,128)(2,1)}, f32[48,768]{1,0:T(8,128)}, f32[6,128]{1,0:T(8,128)}, /*index=5*/f32[6,128]{1,0:T(8,128)}) custom-call(bf16[1024,768]{1,0:T(8,128)(2,1)} %get-tuple-element.12.refs_0_, bf16[1024,768]{1,0:T(8,128)(2,1)} %get-tuple-element.13.refs_1_, ...), custom_call_target="tpu_custom_call" | custom-call | tf_op jit(solution)/shard_map/pallas_call | solution.py:716
